TPU v7x, 32 devices: a whole 2x2x4 slice. The times are simulated.
32 devices in a mesh: row: 4 (over x, core), col: 4 (over z), kern: 2 (over y).
Axes of the slice: x: 2, y: 2, z: 4, core: 2. Of those that a mesh axis runs over, the one named last changes fastest.
Arguments:
- mask_levels: int32 [128, 2048], P('row', 'col'), may hold values from 0 to 3
- level_offset: float32 [128, 2048], P('row', 'col'), may hold values from -6 to 6
- target_bits: int32 [128, 2048], P('row', 'col'), may hold values 0 or 1
- socs_kernels: bfloat16 [2, 24, 35, 35], P(None, 'kern'), may hold values from -0.067871094 to 0.067871094
- kernel_weights: float32 [24], P('kern'), may hold values from 0.1 to 1
Outputs:
- resist_image: float32 [128, 2048], P('row', 'col')
- mask_gradient: float32 [128, 2048], P('row', 'col')
All inputs are finite; a program needn't handle non-finite values. No bound on the sum of `target_bits` on one device may be relied on, other than what follows from the above.
Results may differ from a plain program's by a relative error of at most 0.0039.
Values may be sent and summed in bfloat16 or wider, within the bound.
A program may use at most 64 MiB of HBM per device.

v0:
```python
import jax
import jax.numpy as jnp
from jax import lax
from jax.sharding import PartitionSpec as P

steepness = 4.0
threshold = 1.0
loss_gain = 32.0


def padded_2(value, sides, width):
    for axis, dim in sides:
        size, length = (lax.axis_size(axis), value.shape[dim])
        up = [(i, (i + 1) % size) for i in range(size - 1)]
        down = [(j, i) for i, j in up]
        last = lax.slice_in_dim(value, length - width, length, axis=dim)
        first = lax.slice_in_dim(value, 0, width, axis=dim)
        before = lax.ppermute(last, axis, up)
        after = lax.ppermute(first, axis, down)
        value = jnp.concatenate([before, value, after], axis=dim)
    return value


def column_windows(padded, blocks, reach):
    leading = padded.shape[:-1]
    central = padded[..., : blocks * 128].reshape(leading + (blocks, 128))
    filler = jnp.zeros(leading + (128 - reach,), padded.dtype)
    longer = jnp.concatenate([padded, filler], axis=-1)
    trailing = longer[..., 128:].reshape(leading + (blocks, 128))[..., :reach]
    return jnp.concatenate([central, trailing], axis=-1)


def band_select(stencil):
    window = 128 + stencil - 1
    offsets = (
        jnp.arange(window, dtype=jnp.int32)[:, None, None]
        - jnp.arange(128, dtype=jnp.int32)[None, :, None]
    )
    return (offsets == jnp.arange(stencil, dtype=jnp.int32)[None, None, :]).astype(jnp.bfloat16)


def forward_row(select, kernels, tap_row):
    kernel_row = lax.dynamic_index_in_dim(kernels, tap_row, 2, keepdims=False)
    toeplitz = jnp.einsum("job,ckb->jcko", select, kernel_row, preferred_element_type=jnp.float32)
    return toeplitz.astype(jnp.bfloat16).reshape(select.shape[0], -1)


def adjoint_row(select, flipped, tap_row):
    kernel_row = lax.dynamic_index_in_dim(flipped, tap_row, 2, keepdims=False)
    toeplitz = jnp.einsum("job,ckb->ckjo", select, kernel_row, preferred_element_type=jnp.float32)
    return toeplitz.astype(jnp.bfloat16).reshape(2 * flipped.shape[1], select.shape[0], 128)


def resist_terms(intensity, target):
    resist = jax.nn.sigmoid(steepness * (intensity - threshold))
    slope_term = (
        loss_gain * steepness * (resist - target.astype(jnp.float32)) * resist * (1.0 - resist)
    )
    return (resist, slope_term)


def per_device(mask_levels, level_offset, target_bits, socs_kernels, kernel_weights):
    tile_rows, tile_cols = mask_levels.shape
    stencil = socs_kernels.shape[-1]
    margin = stencil // 2
    reach = 2 * margin
    blocks = tile_cols // 128
    local_kernels = socs_kernels.shape[1]
    channels = 2 * local_kernels
    select = band_select(stencil)
    flipped = socs_kernels[:, :, ::-1, ::-1]
    mask_full = jax.nn.sigmoid(2.0 * (mask_levels.astype(jnp.float32) - 1.5) + level_offset)
    mask_bf = mask_full.astype(jnp.bfloat16)
    padded = padded_2(mask_bf, (("row", 0), ("col", 1)), margin)
    windows = column_windows(padded, blocks, reach)

    def forward_step(tap_row, running):
        row_slab = lax.dynamic_slice_in_dim(windows, tap_row, tile_rows, 0)
        weights_row = forward_row(select, socs_kernels, tap_row)
        return running + jnp.einsum(
            "xnj,jf->xnf", row_slab, weights_row, preferred_element_type=jnp.float32
        )

    fields = lax.fori_loop(
        0, stencil, forward_step, jnp.zeros((tile_rows, blocks, channels * 128), jnp.float32)
    )
    fields = fields.reshape(tile_rows, blocks, 2, local_kernels, 128)
    partial_value = jnp.sum(
        fields * fields * kernel_weights[None, None, None, :, None], axis=(2, 3)
    )
    partial_value = partial_value.reshape(tile_rows, tile_cols)
    intensity = lax.psum(partial_value, "kern")
    resist, slope_term = resist_terms(intensity, target_bits)
    scaled = (
        2.0
        * kernel_weights[None, None, None, :, None]
        * slope_term.reshape(tile_rows, blocks, 1, 1, 128)
    )
    charge = (scaled * fields).astype(jnp.bfloat16)
    charge = jnp.transpose(charge, (2, 3, 0, 1, 4)).reshape(channels, tile_rows, tile_cols)
    charge_padded = padded_2(charge, (("row", 1), ("col", 2)), margin)
    charge_windows = column_windows(charge_padded, blocks, reach)

    def adjoint_step(tap_row, running):
        row_slab = lax.dynamic_slice_in_dim(charge_windows, tap_row, tile_rows, 1)
        weights_row = adjoint_row(select, flipped, tap_row)
        return running + jnp.einsum(
            "cxnj,cjo->xno", row_slab, weights_row, preferred_element_type=jnp.float32
        )

    gradient_part = lax.fori_loop(
        0, stencil, adjoint_step, jnp.zeros((tile_rows, blocks, 128), jnp.float32)
    )
    gradient_part = gradient_part.reshape(tile_rows, tile_cols)
    summed = lax.psum(gradient_part, "kern")
    return (resist, summed * mask_full * (1.0 - mask_full))


def solution(mesh):
    return jax.shard_map(
        per_device,
        mesh=mesh,
        in_specs=(
            P("row", "col"),
            P("row", "col"),
            P("row", "col"),
            P(None, "kern", None, None),
            P("kern"),
        ),
        out_specs=(P("row", "col"), P("row", "col")),
        check_vma=False,
    )
```

profile of v0, /device:TPU:0, one launch (start us, length us, event | category | flops | bytes accessed | tf_op | source)
XLA Modules:
  0.0 439.0 jit_solution(15461233855886850781)
XLA Ops:
  8.1 2.4 collective-permute-start
  11.8 3.9 collective-permute-done.1
  15.8 3.5 collective-permute-start.2
  21.6 3.3 collective-permute-done.3
  25.2 157.3 %while.28 = (s32[]{:T(128)}, f32[32,4,3072]{2,0,1:T(8,128)}, bf16[66,4,162]{2,0,1:T(8,128)(2,1)S(1)}, bf16[2,12,35,35]{3,1,0,2:T(8,128)(2,1)S(1)}, s32[162,128]{1,0:T(8,128)S(1)}, /*index=5*/s32[]{:T(128)}, s32[]{:T(128)}) while((s32[]{:T(128)}, f32[32,4,3072]{2,0,1:T(8,128)}, bf16[66,4,162]{2,0,1:T(8,128)(2,1)S(1)}, ...), condition=%wide.region_1.2_spmd.clone, body=%wide.region_0.1_spmd.clone.sunk | while | flops 164974080 | bytes 9314399 | solution.py:84
  29.9 3.0 convolution_add_fusion.2
  34.4 3.0 convolution_add_fusion.2
  38.9 3.0 convolution_add_fusion.2
  43.5 3.0 convolution_add_fusion.2
  48.0 3.0 convolution_add_fusion.2
  52.5 3.0 convolution_add_fusion.2
  57.0 3.0 convolution_add_fusion.2
  61.6 3.0 convolution_add_fusion.2
  66.1 3.0 convolution_add_fusion.2
  70.6 3.0 convolution_add_fusion.2
  75.2 3.0 convolution_add_fusion.2
  79.7 3.0 convolution_add_fusion.2
  84.3 3.0 convolution_add_fusion.2
  88.8 3.0 convolution_add_fusion.2
  93.3 3.0 convolution_add_fusion.2
  97.9 3.0 convolution_add_fusion.2
  102.4 3.0 convolution_add_fusion.2
  106.9 3.0 convolution_add_fusion.2
  111.5 3.0 convolution_add_fusion.2
  116.0 3.0 convolution_add_fusion.2
  120.5 3.0 convolution_add_fusion.2
  125.1 3.0 convolution_add_fusion.2
  129.6 3.0 convolution_add_fusion.2
  134.1 3.0 convolution_add_fusion.2
  138.7 3.0 convolution_add_fusion.2
  143.2 3.0 convolution_add_fusion.2
  147.7 3.0 convolution_add_fusion.2
  152.3 3.0 convolution_add_fusion.2
  156.8 3.0 convolution_add_fusion.2
  161.3 3.0 convolution_add_fusion.2
  165.9 3.0 convolution_add_fusion.2
  170.4 3.0 convolution_add_fusion.2
  174.9 3.0 convolution_add_fusion.2
  179.5 3.0 convolution_add_fusion.2
  185.6 22.1 %all-reduce.3.cloned.1.call-done = f32[32,512]{1,0:T(8,128)} async-done(((f32[32,512]{1,0:T(8,128)}), f32[32,512]{1,0:T(8,128)}) %all-reduce.3.cloned.1.call-update) | async-done | bytes 65552 | tf_op jit(solution)/shard_map/psum | solution.py:92
  214.1 3.8 collective-permute-done.5
  219.1 3.4 collective-permute-start.6
  224.9 3.7 collective-permute-done.6
  229.4 3.4 collective-permute-done.7
  232.8 6.0 %pad_maximum_fusion.4 = (bf16[24,66,512]{2,1,0:T(8,128)(2,1)S(1)}, bf16[24,66,512]{2,1,0:T(8,128)(2,1)}) fusion(bf16[24,66,17]{2,1,0:T(8,128)(2,1)} %copy-done.1, bf16[24,17,512]{2,1,0:T(8,128)(2,1)} %copy-done, bf16[24,32,512]{2,1,0:T(8,128)(2,1)S(1)} %reshape.72, bf16[24,17,512]{2,1,0:T(8,128)(2,1)S(1)} %copy.51, bf16[512]{0:T(512)(128)(2,1)S(1)} %pad_slice_fusion, ...), kind=kLoop, calls=%fused_computation.36 | loop fusion | flops 14598144 | bytes 4974784 | tf_op jit(solution)/shard_map/concatenate | solution.py:20
  238.8 3.7 reshape.86
  244.6 5.5 %pad_maximum_fusion = bf16[24,66,4,162]{3,2,1,0:T(4,128)(2,1)} fusion(bf16[24,66,4,34]{3,2,1,0:T(4,128)(2,1)} %bitcast.76, bf16[24,66,4,128]{3,2,1,0:T(4,128)(2,1)} %reshape.85), kind=kLoop, calls=%fused_computation.29 | loop fusion | flops 4105728 | bytes 4105728 | tf_op jit(solution)/shard_map/concatenate | solution.py:30
  250.1 155.4 %while.29 = (s32[]{:T(128)}, f32[32,4,128]{2,0,1:T(8,128)S(1)}, bf16[24,66,4,162]{3,2,1,0:T(4,128)(2,1)}, bf16[2,12,35,35]{3,1,0,2:T(8,128)(2,1)}, s32[162,128]{1,0:T(8,128)S(1)}, /*index=5*/s32[]{:T(128)}, s32[]{:T(128)}) while((s32[]{:T(128)}, f32[32,4,128]{2,0,1:T(8,128)S(1)}, bf16[24,66,4,162]{3,2,1,0:T(4,128)(2,1)}, ...), condition=%wide.region_5.6_spmd.clone, body=%wide.region_4.5_spmd.clone.sunk | while | flops 164220416 | bytes 7190107 | solution.py:111
  251.7 2.2 constant_dynamic-slice_fusion.2
  256.1 2.2 constant_dynamic-slice_fusion.2
  260.6 2.2 constant_dynamic-slice_fusion.2
  265.0 2.2 constant_dynamic-slice_fusion.2
  269.5 2.2 constant_dynamic-slice_fusion.2
  273.9 2.2 constant_dynamic-slice_fusion.2
  278.3 2.2 constant_dynamic-slice_fusion.2
  282.8 2.2 constant_dynamic-slice_fusion.2
  287.2 2.2 constant_dynamic-slice_fusion.2
  291.7 2.2 constant_dynamic-slice_fusion.2
  296.1 2.2 constant_dynamic-slice_fusion.2
  300.6 2.2 constant_dynamic-slice_fusion.2
  305.0 2.2 constant_dynamic-slice_fusion.2
  309.4 2.2 constant_dynamic-slice_fusion.2
  313.9 2.2 constant_dynamic-slice_fusion.2
  406.2 24.4 %all-reduce.5.cloned.1.call-done = f32[32,512]{1,0:T(8,128)} async-done(((f32[32,512]{1,0:T(8,128)}), f32[32,512]{1,0:T(8,128)}) %all-reduce.5.cloned.1.call-update) | async-done | bytes 65552 | tf_op jit(solution)/shard_map/psum | solution.py:115
  (290 shorter events, 197.8 us)
Async XLA Ops:
  7.2 200.5 %all-reduce.3.cloned.1.call-start = ((), (), s32[]{:S(2)}) async-start(), calls=%async_computation | async-start | bytes 131072 | tf_op jit(solution)/shard_map/psum | solution.py:92
  8.1 3.7 collective-permute-start
  10.5 5.2 %collective-permute-start.1 = (bf16[17,512]{1,0:T(8,128)(2,1)S(1)}, bf16[17,512]{1,0:T(8,128)(2,1)S(1)}, u32[]{:S(2)}, u32[]{:S(2)}) collective-permute-start(bf16[17,512]{1,0:T(8,128)(2,1)S(1)} %get-tuple-element.302), channel_id=1, source_target_pairs={{8,0},{16,8},{24,16},{9,1},{17,9},{25,17},{10,2},{18,10},{26,18},{... | collective-permute-start | bytes 52232 | tf_op jit(solution)/shard_map/ppermute | solution.py:19
  15.8 5.9 %collective-permute-start.2 = (bf16[66,17]{1,0:T(8,128)(2,1)S(1)}, bf16[66,17]{1,0:T(8,128)(2,1)S(1)}, u32[]{:S(2)}, u32[]{:S(2)}) collective-permute-start(bf16[66,17]{1,0:T(8,128)(2,1)S(1)} %get-tuple-element.299), channel_id=1, source_target_pairs={{0,2},{2,4},{4,6},{1,3},{3,5},{5,7},{8,10},{10,12},{12,14},{9,11},... | collective-permute-start | bytes 6740 | tf_op jit(solution)/shard_map/ppermute | solution.py:18
  19.3 5.7 %collective-permute-start.3 = (bf16[66,17]{1,0:T(8,128)(2,1)S(1)}, bf16[66,17]{1,0:T(8,128)(2,1)S(1)}, u32[]{:S(2)}, u32[]{:S(2)}) collective-permute-start(bf16[66,17]{1,0:T(8,128)(2,1)S(1)} %get-tuple-element.300), channel_id=1, source_target_pairs={{2,0},{4,2},{6,4},{3,1},{5,3},{7,5},{10,8},{12,10},{14,12},{11,9},... | collective-permute-start | bytes 6740 | tf_op jit(solution)/shard_map/ppermute | solution.py:19
  182.5 1.7 copy-start.5
  184.2 23.4 %copy-start.4 = (s32[32,512]{1,0:T(8,128)S(1)}, s32[32,512]{1,0:T(8,128)}, u32[]{:S(2)}) copy-start(s32[32,512]{1,0:T(8,128)} %param.11) | copy-start | bytes 196612
  185.5 245.1 %all-reduce.5.cloned.1.call-start = ((), (), s32[]{:S(2)}) async-start(), calls=%async_computation.1 | async-start | bytes 131072 | tf_op jit(solution)/shard_map/psum | solution.py:115
  211.1 2.8 collective-permute-start.4
  212.6 5.3 %collective-permute-start.5 = (bf16[24,17,512]{2,0,1:T(8,128)(2,1)S(1)}, bf16[24,17,512]{2,0,1:T(8,128)(2,1)S(1)}, u32[]{:S(2)}, u32[]{:S(2)}) collective-permute-start(bf16[24,17,512]{2,0,1:T(8,128)(2,1)S(1)} %copy.50), channel_id=1, source_target_pairs={{8,0},{16,8},{24,16},{9,1},{17,9},{25,17},{10,2},{18,10},{26,18},{... | collective-permute-start | bytes 1253384 | tf_op jit(solution)/shard_map/ppermute | solution.py:19
  218.0 10.5 %copy-start = (bf16[24,17,512]{2,1,0:T(8,128)(2,1)}, bf16[24,17,512]{2,1,0:T(8,128)(2,1)S(1)}, u32[]{:S(2)}) copy-start(bf16[24,17,512]{2,1,0:T(8,128)(2,1)S(1)} %copy.52) | copy-start | bytes 1253380
  219.1 9.5 %collective-permute-start.6 = (bf16[24,66,17]{2,1,0:T(8,128)(2,1)}, bf16[24,66,17]{2,1,0:T(8,128)(2,1)S(1)}, u32[]{:S(2)}, u32[]{:S(2)}) collective-permute-start(bf16[24,66,17]{2,1,0:T(8,128)(2,1)} %get-tuple-element.293), channel_id=1, source_target_pairs={{0,2},{2,4},{4,6},{1,3},{3,5},{5,7},{8,10},{10,12},{12,14},{9,11},... | collective-permute-start | bytes 161576 | tf_op jit(solution)/shard_map/ppermute | solution.py:18
  222.5 10.3 %collective-permute-start.7 = (bf16[24,66,17]{2,1,0:T(8,128)(2,1)S(1)}, bf16[24,66,17]{2,1,0:T(8,128)(2,1)}, u32[]{:S(2)}, u32[]{:S(2)}) collective-permute-start(bf16[24,66,17]{2,1,0:T(8,128)(2,1)S(1)} %get-tuple-element.294), channel_id=1, source_target_pairs={{2,0},{4,2},{6,4},{3,1},{5,3},{7,5},{10,8},{12,10},{14,12},{11,9},... | collective-permute-start | bytes 161576 | tf_op jit(solution)/shard_map/ppermute | solution.py:19
  228.6 0.8 copy-start.1
  250.1 180.6 %copy-start.2 = (f32[32,512]{1,0:T(8,128)S(1)}, f32[32,512]{1,0:T(8,128)}, u32[]{:S(2)}) copy-start(f32[32,512]{1,0:T(8,128)} %param.10) | copy-start | bytes 196612
  250.1 180.6 %copy-start.3 = (s32[32,512]{1,0:T(8,128)S(1)}, s32[32,512]{1,0:T(8,128)}, u32[]{:S(2)}) copy-start(s32[32,512]{1,0:T(8,128)} %param.9) | copy-start | bytes 196612
Sparse Core Ops, SparseCore 0:
  185.6 21.9 all-reduce.2
  406.3 24.2 all-reduce.4
where the time goes:
time: 443 us; the launch traced here: 439 us
  matrix products  192 us (43%)
  local copies, waits for them, and re-layouts  132 us (30%)
  waiting for transfers between devices  64.7 us (15%)
  other arithmetic  18 us (4%)
  starting transfers between devices  16 us (4%)
  between operations  14.3 us (3%)
    dot_general x35, matrix products, forward_step(): jnp.einsum('xnj,jf->xnf', row_slab, weights_row, preferred_element_type=j...  103 us
    dynamic_slice x35, local copies, waits for them, and re-layouts, adjoint_step(): row_slab = lax.dynamic_slice_in_dim(charge_windows, tap_row, tile_rows, 1)  77.8 us
    dot_general x35, matrix products, adjoint_row(): jnp.einsum('job,ckb->ckjo', select, kernel_row, preferred_element_type=jn...  46.3 us
    psum x1, waiting for transfers between devices, per_device(): summed = lax.psum(gradient_part, 'kern')  24.4 us
    reshape x35, local copies, waits for them, and re-layouts, forward_row(): return toeplitz.astype(jnp.bfloat16).reshape(select.shape[0], -1)  23.3 us
    psum x1, waiting for transfers between devices, per_device(): intensity = lax.psum(partial_value, 'kern')  22.1 us
    dot_general x35, matrix products, forward_row(): jnp.einsum('job,ckb->jcko', select, kernel_row, preferred_element_type=jn...  21.6 us
    dot_general x35, matrix products, adjoint_step(): jnp.einsum('cxnj,cjo->xno', row_slab, weights_row, preferred_element_type...  20.4 us
  transfers between devices with their start and end apart: 10, of which 7 were waited for; matrix products, arithmetic and copies ran while one was open for 1% of the time, Pallas kernels for 0%

commit v1 on v0

v1 whole, which is shorter than its diff:
```python
import functools

import jax
import jax.numpy as jnp
from jax import lax
from jax.experimental import pallas as pl
from jax.experimental.pallas import tpu as pltpu
from jax.sharding import PartitionSpec as P

MESH = pl.DeviceIdType.MESH
F32 = jnp.float32
BF = jnp.bfloat16
TAPS = 35
HALF = 17
BY = 16
SLOT = BY + TAPS - 1
TALL = 5
STEPS = 7
CHUNK = 64
PART = 128


def sigmoid(value):
    return 1.0 / (1.0 + jnp.exp(-value))


def lane_of(shape):
    return lax.broadcasted_iota(jnp.int32, shape, 1)


def split_dot(value, picks):
    high = value.astype(BF)
    low = (value - high.astype(F32)).astype(BF)
    return jnp.dot(high, picks, preferred_element_type=F32) + jnp.dot(
        low, picks, preferred_element_type=F32
    )


def kernel(R, C, KN, levels_ref, offset_ref, target_ref, kern_ref, weight_ref,
           resist_ref, grad_ref, full_s, send_s, center_s, edge_s, taps_s, own_s, kern_s, kernx_s,
           weight_s, weightx_s, fields_s, charge_s,
           toep_s, image_s, tgt_s, qa_s, qb_s, rcomp_s, acc_s, adj_s, outsend_s, outrecv_s,
           msend, mrecv, esend, erecv, ksend, krecv, wsend, wrecv, osend, orecv):
    TR, TC = levels_ref.shape
    NX = R * TR
    G = R * KN
    ST = TC // G
    HALF_K = weight_ref.shape[1]
    CH = 2 * HALF_K
    groups = -(-(ST + 2 * HALF) // BY)
    tiles = TC // 128
    lead = 128 - 2 * HALF
    r, c, k = (lax.axis_index(name) for name in ("row", "col", "kern"))
    me = k * R + r
    first = [i for i in range(G) if (ST * i + lead) // 128 == 0]
    last = [i for i in range(G) if (ST * i + lead) // 128 == tiles]

    barrier = pltpu.get_barrier_semaphore()
    for d in range(1, G):
        peer = lax.rem(me + d, G)
        pl.semaphore_signal(barrier, inc=1, device_id=(lax.rem(peer, R), c, peer // R),
                            device_id_type=MESH)
    waits = jnp.int32(G - 1)
    for needy, step in ((first, 1), (last, -1)):
        for i in needy:
            has = (c + step >= 0) & (c + step < C) & (k == i // R)
            gets = (c - step >= 0) & (c - step < C) & (me == i)

            @pl.when(has)
            def _():
                pl.semaphore_signal(barrier, inc=1, device_id=(i % R, c + step, i // R),
                                    device_id_type=MESH)

            @pl.when(gets)
            def _():
                for rr in range(R):
                    pl.semaphore_signal(barrier, inc=1, device_id=(rr, c - step, k),
                                        device_id_type=MESH)

            waits = waits + jnp.where(has, 1, 0) + jnp.where(gets, R, 0)

    full = sigmoid(2.0 * (levels_ref[...].astype(F32) - 1.5) + offset_ref[...])
    full_s[...] = full
    send_s[0] = full.astype(BF)
    send_s[1] = target_ref[...].astype(F32).astype(BF)
    weight_s[...] = jnp.zeros((8, 128), F32)
    weight_s[0:1, 0:HALF_K] = weight_ref[...]

    pl.semaphore_wait(barrier, waits)

    def window(i):
        tile = (ST * i + lead) // 128
        return pl.multiple_of((jnp.clip(tile, 1, tiles - 1) - 1) * 128, 128)

    other = (r, c, 1 - k)
    kcopy = pltpu.make_async_remote_copy(kern_s, kernx_s, ksend, krecv,
                                         device_id=other, device_id_type=MESH)
    wcopy = pltpu.make_async_remote_copy(weight_s, weightx_s, wsend, wrecv,
                                         device_id=other, device_id_type=MESH)
    mcopies = []
    for d in range(1, R):
        rr = lax.rem(r + d, R)
        copy = pltpu.make_async_remote_copy(
            send_s.at[:, :, pl.ds(window(k * R + rr), 256)], center_s.at[r],
            msend.at[d - 1], mrecv.at[r], device_id=(rr, c, k), device_id_type=MESH)
        copy.start()
        mcopies.append(copy)

    def edge_copy(i, step, n, sender_row):
        low = TC - 128 if step == 1 else 0
        return pltpu.make_async_remote_copy(
            send_s.at[:, :, pl.ds(low, 128)], edge_s.at[sender_row],
            esend.at[n], erecv.at[sender_row],
            device_id=(i % R, c + step, i // R), device_id_type=MESH)

    edges = [(i, 1) for i in first] + [(i, -1) for i in last]
    for n, (i, step) in enumerate(edges):
        @pl.when((c + step >= 0) & (c + step < C) & (k == i // R))
        def _():
            edge_copy(i, step, n, r).start()
    wcopy.start()

    WIDE = STEPS * 256
    taps_s[...] = jnp.zeros(taps_s.shape, F32)
    for part in range(2):
        for n in range(HALF_K):
            base = (part * HALF_K + n) * 40
            taps_s[base : base + TAPS, 0:TAPS] = kern_ref[part, n].astype(F32)
    for t in range(STEPS):
        low = jnp.zeros((CH, 128), F32)
        high = jnp.zeros((CH, 128), F32)
        for q in range(TALL):
            taps = taps_s[pl.ds(t * TALL + q, CH, stride=40), :]
            begin = q * SLOT
            moved = taps if begin == 0 else pltpu.roll(taps, begin % 128, 1)
            lane = lane_of((CH, 128))
            if begin + TAPS <= 128:
                low = low + moved
            elif begin >= 128:
                high = high + moved
            else:
                low = low + jnp.where(lane >= begin, moved, 0.0)
                high = high + jnp.where(lane < begin, moved, 0.0)
        own_s[:, t * 256 : t * 256 + 128] = low
        own_s[:, t * 256 + 128 : t * 256 + 256] = high
    kern_s[:, 0:WIDE] = own_s[0:16, :].astype(BF)
    kern_s[:, WIDE:] = jnp.concatenate(
        [own_s[16:24, : WIDE // 2], own_s[16:24, WIDE // 2 :]], axis=0).astype(BF)
    kcopy.start()

    center_s[r] = send_s[:, :, pl.ds(window(me), 256)]
    image_s[0 : HALF * 8, :] = jnp.zeros((HALF * 8, 128), F32)
    tail = image_s.shape[0] - (HALF + NX) * 8
    image_s[(HALF + NX) * 8 :, :] = jnp.zeros((tail, 128), F32)
    acc_s[...] = jnp.zeros(acc_s.shape, F32)

    def build(group, base):
        for o in range(BY):
            moved = base if o == 0 else pltpu.roll(base, o, 1)
            toep_s[group * 256 + o * 16 : group * 256 + o * 16 + 16, :] = moved.astype(BF)

    build(0, own_s[0:16, :])

    for d in range(1, R):
        rr = lax.rem(r + d, R)
        pltpu.make_async_remote_copy(
            send_s.at[:, :, pl.ds(0, 256)], center_s.at[rr], msend.at[d - 1], mrecv.at[rr],
            device_id=(rr, c, k), device_id_type=MESH).wait_recv()
    for n, (i, step) in enumerate(edges):
        @pl.when((c - step >= 0) & (c - step < C) & (me == i))
        def _():
            for rr in range(R):
                edge_copy(i, step, n, rr).wait_recv()

    start = ST * me + lead
    tile = start // 128
    off = start - tile * 128
    is_first, is_last = tile == 0, tile == tiles
    col0 = c * TC + me * ST - 2 * HALF
    column = lane_of((TR, 256)) + col0
    inside = (column >= 0) & (column < C * TC)
    for rr in range(R):
        for part in range(2):
            mid = center_s[rr, part].astype(F32)
            side = edge_s[rr, part].astype(F32)
            a0, a1 = mid[:, :128], mid[:, 128:]
            t0 = jnp.where(is_first, side, jnp.where(is_last, a1, a0))
            t1 = jnp.where(is_first, a0, jnp.where(is_last, side, a1))
            both = jnp.concatenate([t0, t1], axis=1)
            view = jnp.where(inside, pltpu.roll(both, 256 - off, 1), 0.0)
            for g in range(groups):
                shift = BY * g + (0 if part == 0 else HALF)
                moved = view if shift == 0 else pltpu.roll(view, 256 - shift, 1)
                if part == 0:
                    image_s[pl.ds((HALF + TR * rr) * 8 + g, TR, stride=8), :] = moved[:, :128]
                else:
                    tgt_s[pl.ds(TR * rr * 8 + g, TR, stride=8), :] = moved[:, :128]

    def pack(n, carry):
        base = pl.multiple_of(n * 128, 128)
        rows = image_s[pl.ds(base, 22 * 8), :]
        lane = lane_of((17 * 8, 128))

        def slot(s, by):
            moved = rows if by == 0 else pltpu.roll(rows, by, 1)
            return moved[s * 8 : (s + 17) * 8]

        two = slot(2, 2 * SLOT)
        low = jnp.where(lane < SLOT, slot(0, 0), jnp.where(lane < 2 * SLOT, slot(1, SLOT), two))
        high = jnp.where(
            lane < 3 * SLOT - 128, two,
            jnp.where(lane < 4 * SLOT - 128, slot(3, 3 * SLOT - 128),
                      jnp.where(lane < 5 * SLOT - 128, slot(4, 4 * SLOT - 128), 0.0)))
        value = jnp.concatenate([low, high], axis=1)
        qa_s[pl.ds(base, 128), :] = value[:128].astype(BF)
        qb_s[pl.ds(base, 128), :] = value[8:].astype(BF)
        return carry

    lax.fori_loop(0, (NX + 32) // 16, pack, 0)

    kcopy.wait_recv()
    wcopy.wait_recv()
    theirs = kernx_s[:, 0:WIDE].astype(F32)
    rest = kernx_s[:, WIDE:].astype(F32)
    build(1, jnp.concatenate([own_s[16:24, :], theirs[0:8]], axis=0))
    build(2, jnp.concatenate(
        [theirs[8:16], jnp.concatenate([rest[0:8], rest[8:16]], axis=1)], axis=0))

    lane8 = lane_of((8, 128))
    mine, other_w = weight_s[...], weightx_s[...]
    channel_w = (mine + pltpu.roll(mine, HALF_K, 1) + pltpu.roll(other_w, CH, 1)
                 + pltpu.roll(other_w, CH + HALF_K, 1))
    weights = []
    for group in range(3):
        piece = channel_w if group == 0 else pltpu.roll(channel_w, 128 - 16 * group, 1)
        piece = jnp.where(lane8 < 16, piece, 0.0)
        for by in (16, 32, 64):
            piece = piece + pltpu.roll(piece, by, 1)
        weights.append(jnp.concatenate([piece, piece], axis=1)[0:1])

    M = CHUNK * 8
    gather = (lax.broadcasted_iota(jnp.int32, (256, 128), 0) // 16
              == lax.broadcasted_iota(jnp.int32, (256, 128), 1)).astype(F32).astype(BF)
    spread = (lax.broadcasted_iota(jnp.int32, (128, 256), 0)
              == lax.broadcasted_iota(jnp.int32, (128, 256), 1) // 16).astype(F32).astype(BF)
    group_at = lax.rem(lax.broadcasted_iota(jnp.int32, (PART, 128), 0), 8)
    field_col = lane_of((PART, 128)) + BY * group_at + (col0 + HALF)
    live = ((lane_of((PART, 128)) < BY) & (group_at < groups)
            & (field_col >= 0) & (field_col < C * TC))

    def forward(n):
        row0 = n * M
        pieces = []
        for t in range(STEPS):
            source = qa_s if t % 2 == 0 else qb_s
            at = row0 + (TALL * t - t % 2) * 8
            pieces.append(source[at : at + M, :])
        patches = jnp.concatenate(pieces, axis=1)
        for group in range(3):
            fields_s[row0 : row0 + M, group * 256 : (group + 1) * 256] = lax.dot_general(
                patches, toep_s[group * 256 : (group + 1) * 256, :],
                (((1,), (1,)), ((), ())), preferred_element_type=F32)

    def middle(n):
        for at in range(n * M, (n + 1) * M, PART):
            rows = slice(at, at + PART)
            power = None
            for group in range(3):
                f = fields_s[rows, group * 256 : (group + 1) * 256]
                term = weights[group] * f * f
                power = term if power is None else power + term
            resist = sigmoid(4.0 * (split_dot(power, gather) - 1.0))
            slope = jnp.where(
                live, 128.0 * (resist - tgt_s[rows, :]) * resist * (1.0 - resist), 0.0)
            rcomp_s[rows, :] = jnp.where(live, resist, 0.0)
            wide = split_dot(slope, spread)
            for group in range(3):
                cols = slice(group * 256, (group + 1) * 256)
                charge_s[rows, cols] = (
                    2.0 * weights[group] * wide * fields_s[rows, cols]).astype(BF)

    def backward(n):
        for t in range(STEPS):
            at = n * M + TALL * t * 8
            acc_s[at : at + M, :] += jnp.dot(
                charge_s[n * M : (n + 1) * M, :], toep_s[:, t * 256 : (t + 1) * 256],
                preferred_element_type=F32)

    fold = 128 // ST
    piece_rows = TR // fold

    def send_out(part, source, margin):
        for rr in range(R):
            total = None
            for g in range(groups):
                value = source[pl.ds(TR * rr * 8 + g, TR, stride=8), :]
                by = (BY * g - margin) % 128
                value = value if by == 0 else pltpu.roll(value, by, 1)
                total = value if total is None else total + value
            lane = lane_of((piece_rows, 128))
            packed = total[0:piece_rows]
            for q in range(1, fold):
                moved = pltpu.roll(total[q * piece_rows : (q + 1) * piece_rows], q * ST, 1)
                packed = jnp.where(lane < q * ST, packed, moved)
            outsend_s[part, rr] = packed
        copies = []
        for d in range(1, G):
            peer = lax.rem(me + d, G)
            copy = pltpu.make_async_remote_copy(
                outsend_s.at[part, lax.rem(peer, R)], outrecv_s.at[part, me],
                osend.at[part, d - 1], orecv.at[part, me],
                device_id=(lax.rem(peer, R), c, peer // R), device_id_type=MESH)
            copy.start()
            copies.append(copy)
        outrecv_s[part, me] = outsend_s[part, r]
        return copies

    chunks = NX // CHUNK
    forward(0)
    for n in range(chunks):
        if n + 1 < chunks:
            forward(n + 1)
        middle(n)
        if n + 1 < chunks:
            backward(n)
    ocopies = send_out(0, rcomp_s, HALF)
    backward(chunks - 1)

    def unpack(n, carry):
        base = pl.multiple_of((n * 16 + HALF - 4) * 8, 8)
        low = acc_s[pl.ds(base, 20 * 8), 0:128]
        high = acc_s[pl.ds(base, 20 * 8), 128:256]
        lane = lane_of((128, 128))

        def slot(value, s, by):
            moved = value if by == 0 else pltpu.roll(value, by, 1)
            return moved[(4 - s) * 8 : (20 - s) * 8]

        two = jnp.where(lane < 128 - 2 * SLOT, slot(low, 2, 128 - 2 * SLOT),
                        slot(high, 2, 128 - 2 * SLOT))
        total = (slot(low, 0, 0) + slot(low, 1, 128 - SLOT) + two
                 + slot(high, 3, 256 - 3 * SLOT) + slot(high, 4, 256 - 4 * SLOT))
        adj_s[pl.ds(pl.multiple_of(n * 128, 128), 128), :] = jnp.where(lane < SLOT, total, 0.0)
        return carry

    lax.fori_loop(0, NX // 16, unpack, 0)

    ocopies += send_out(1, adj_s, 2 * HALF)

    def receive(part):
        for d in range(1, G):
            peer = lax.rem(me + d, G)
            pltpu.make_async_remote_copy(
                outsend_s.at[part, r], outrecv_s.at[part, peer], osend.at[part, d - 1],
                orecv.at[part, peer],
                device_id=(lax.rem(peer, R), c, peer // R), device_id_type=MESH).wait_recv()

    lane = lane_of((piece_rows, 128))
    for part in range(2):
        receive(part)
        for p in range(tiles):
            for q in range(fold):
                rows = slice(q * piece_rows, (q + 1) * piece_rows)
                cols = slice(p * 128, (p + 1) * 128)
                merged = None
                for m in range(fold):
                    value = outrecv_s[part, p * fold + m]
                    by = ((m - q) * ST) % 128
                    value = value if by == 0 else pltpu.roll(value, by, 1)
                    merged = value if m == 0 else jnp.where(lane < m * ST, merged, value)
                if part == 0:
                    resist_ref[rows, cols] = merged
                else:
                    mask = full_s[rows, cols]
                    grad_ref[rows, cols] = merged * mask * (1.0 - mask)

    for copy in mcopies + ocopies:
        copy.wait_send()
    kcopy.wait_send()
    wcopy.wait_send()
    for n, (i, step) in enumerate(edges):
        @pl.when((c + step >= 0) & (c + step < C) & (k == i // R))
        def _():
            edge_copy(i, step, n, r).wait_send()


def per_device(sizes, mask_levels, level_offset, target_bits, socs_kernels, kernel_weights):
    R, C, KN = sizes
    TR, TC = mask_levels.shape
    NX = R * TR
    G = R * KN
    local = socs_kernels.shape[1]
    fold = 128 * G // TC
    vmem = pl.BlockSpec(memory_space=pltpu.VMEM)
    ends = 2 * max(1, R)
    out = jax.ShapeDtypeStruct((TR, TC), F32)
    return pl.pallas_call(
        functools.partial(kernel, R, C, KN),
        out_shape=(out, out),
        in_specs=[vmem] * 5,
        out_specs=(vmem, vmem),
        scratch_shapes=[
            pltpu.VMEM((TR, TC), F32),
            pltpu.VMEM((2, TR, TC), BF),
            pltpu.VMEM((R, 2, TR, 256), BF),
            pltpu.VMEM((R, 2, TR, 128), BF),
            pltpu.VMEM((2 * local * 40, 128), F32),
            pltpu.VMEM((2 * local, STEPS * 256), F32),
            pltpu.VMEM((16, STEPS * 384), BF),
            pltpu.VMEM((16, STEPS * 384), BF),
            pltpu.VMEM((8, 128), F32),
            pltpu.VMEM((8, 128), F32),
            pltpu.VMEM((NX * 8, 768), F32),
            pltpu.VMEM((NX * 8, 768), BF),
            pltpu.VMEM((768, STEPS * 256), BF),
            pltpu.VMEM(((NX + 40) * 8, 128), F32),
            pltpu.VMEM((NX * 8, 128), F32),
            pltpu.VMEM(((NX + 32) * 8, 256), BF),
            pltpu.VMEM(((NX + 32) * 8, 256), BF),
            pltpu.VMEM((NX * 8, 128), F32),
            pltpu.VMEM(((NX + 40) * 8, 256), F32),
            pltpu.VMEM((NX * 8, 128), F32),
            pltpu.VMEM((2, R, TR // fold, 128), F32),
            pltpu.VMEM((2, G, TR // fold, 128), F32),
            pltpu.SemaphoreType.DMA((R,)),
            pltpu.SemaphoreType.DMA((R,)),
            pltpu.SemaphoreType.DMA((ends,)),
            pltpu.SemaphoreType.DMA((R,)),
            pltpu.SemaphoreType.DMA,
            pltpu.SemaphoreType.DMA,
            pltpu.SemaphoreType.DMA,
            pltpu.SemaphoreType.DMA,
            pltpu.SemaphoreType.DMA((2, G)),
            pltpu.SemaphoreType.DMA((2, G)),
        ],
        compiler_params=pltpu.CompilerParams(
            collective_id=0, has_side_effects=True, vmem_limit_bytes=48 * 1024 * 1024),
    )(mask_levels, level_offset, target_bits, socs_kernels, kernel_weights[None])


def solution(mesh):
    sizes = tuple(mesh.shape[name] for name in ("row", "col", "kern"))
    return jax.shard_map(
        functools.partial(per_device, sizes),
        mesh=mesh,
        in_specs=(
            P("row", "col"),
            P("row", "col"),
            P("row", "col"),
            P(None, "kern", None, None),
            P("kern"),
        ),
        out_specs=(P("row", "col"), P("row", "col")),
        check_vma=False,
    )
```

time: 443 us -> 24.5 us (0.06)
  matrix products: 192 us -> 0 us
  local copies, waits for them, and re-layouts: 132 us -> 2.31 us
  waiting for transfers between devices: 64.7 us -> 0 us
  Pallas kernels: 0 us -> 21.3 us
  other arithmetic: 18 us -> 0 us
  starting transfers between devices: 16 us -> 0 us
  between operations: 14.3 us -> 0.71 us
    dot_general x140 -> x0, matrix products: 192 us -> none  [the longest x35 103 us: forward_step(): jnp.einsum('xnj,jf->xnf', row_slab, weights_row, preferred_element_type=j...]
    dynamic_slice x35 -> x0, local copies, waits for them, and re-layouts: 77.8 us -> none  [adjoint_step(): row_slab = lax.dynamic_slice_in_dim(charge_windows, tap_row, tile_rows, 1)]
    psum x2 -> x0, waiting for transfers between devices: 46.5 us -> none  [the longest x1 24.4 us: per_device(): summed = lax.psum(gradient_part, 'kern')]
    reshape x44 -> x0, local copies, waits for them, and re-layouts: 32.4 us -> none  [the longest x35 23.3 us: forward_row(): return toeplitz.astype(jnp.bfloat16).reshape(select.shape[0], -1)]
    pallas_call x0 -> x1, Pallas kernels: none -> 21.3 us  [per_device(): pl.pallas_call(functools.partial(kernel, R, C, KN), out_shape=(out, out),...]
    ppermute x8 -> x0, waiting for transfers between devices: 18.1 us -> none  [the longest x4 14.4 us: padded_2(): after = lax.ppermute(first, axis, down)]
    convert_element_type x70 -> x0, local copies, waits for them, and re-layouts: 17.3 us -> none  [the longest x35 9.23 us: adjoint_row(): toeplitz.astype(jnp.bfloat16)]
    ppermute x8 -> x0, starting transfers between devices: 15.9 us -> none  [the longest x4 10.6 us: padded_2(): before = lax.ppermute(last, axis, up)]
  transfers between devices with their start and end apart: 10 -> 0, of which waited for: 7 -> 0; matrix products, arithmetic and copies ran while one was open for 1% -> 0% of each run, Pallas kernels for 0% -> 0%
where the time goes in v1:
time: 24.5 us; the launch traced here: 24.4 us
  Pallas kernels  21.3 us (87%)
  local copies, waits for them, and re-layouts  2.31 us (9%)
  between operations  0.71 us (3%)
    pallas_call x1, Pallas kernels, per_device(): pl.pallas_call(functools.partial(kernel, R, C, KN), out_shape=(out, out),...  21.3 us
    unnamed x11, local copies, waits for them, and re-layouts  2.31 us

profile of v1, /device:TPU:0, one launch (start us, length us, event | category | flops | bytes accessed | tf_op | source)
XLA Modules:
  0.0 24.4 jit_solution(6281186602868076180)
XLA Ops:
  0.6 0.0 copy-start
  0.6 0.0 copy-start.1
  0.7 0.0 copy-start.2
  0.7 0.0 copy-start.3
  0.7 1.0 %copy.7.kern_ref = bf16[2,12,35,35]{3,2,1,0:T(8,128)(2,1)S(1)} copy(bf16[2,12,35,35]{3,0,2,1:T(2,128)(2,1)} %param.8) | data formatting | bytes 117600 | tf_op args[3]
  1.7 0.0 copy-done
  1.7 0.0 copy-done.1
  1.7 0.0 copy-done.2
  1.7 0.0 copy-done.3
  1.8 21.3 %shard_map.68 = (f32[32,512]{1,0:T(8,128)S(1)}, f32[32,512]{1,0:T(8,128)S(1)}) custom-call(s32[32,512]{1,0:T(8,128)S(1)} %copy-done, f32[32,512]{1,0:T(8,128)S(1)} %copy-done.1, s32[32,512]{1,0:T(8,128)S(1)} %copy-done.2, bf16[2,12,35,35]{3,2,1,0:T(8,128)(2,1)S(1)} %copy.7.kern_ref, f32[1,12]{1,0:T(1,128)S(1)} %bitcast.1), custom_call_target="tpu_custom_call" | custom-call | tf_op jit(solution)/shard_map/pallas_call | solution.py:397
  23.1 0.6 %copy.10 = f32[32,512]{1,0:T(8,128)} copy(f32[32,512]{1,0:T(8,128)S(1)} %get-tuple-element.4) | data formatting | bytes 131072
  23.7 0.6 %copy.11 = f32[32,512]{1,0:T(8,128)} copy(f32[32,512]{1,0:T(8,128)S(1)} %get-tuple-element.5) | data formatting | bytes 131072
Async XLA Ops:
  0.6 1.1 %copy-start = (s32[32,512]{1,0:T(8,128)S(1)}, s32[32,512]{1,0:T(8,128)}, u32[]{:S(2)}) copy-start(s32[32,512]{1,0:T(8,128)} %levels_ref.1) | copy-start | bytes 196612
  0.6 1.1 %copy-start.1 = (f32[32,512]{1,0:T(8,128)S(1)}, f32[32,512]{1,0:T(8,128)}, u32[]{:S(2)}) copy-start(f32[32,512]{1,0:T(8,128)} %offset_ref.1) | copy-start | bytes 196612
  0.7 1.1 %copy-start.2 = (s32[32,512]{1,0:T(8,128)S(1)}, s32[32,512]{1,0:T(8,128)}, u32[]{:S(2)}) copy-start(s32[32,512]{1,0:T(8,128)} %target_ref.1) | copy-start | bytes 196612
  0.7 1.1 %copy-start.3 = (f32[12]{0:T(128)S(1)}, f32[12]{0:T(128)}, u32[]{:S(2)}) copy-start(f32[12]{0:T(128)} %param.9) | copy-start | bytes 148

commit v2 on v1

--- a/solution.py
+++ b/solution.py
@@ -37,7 +37,7 @@
 
 
 def kernel(R, C, KN, levels_ref, offset_ref, target_ref, kern_ref, weight_ref,
-           resist_ref, grad_ref, full_s, send_s, center_s, edge_s, taps_s, own_s, kern_s, kernx_s,
+           out_ref, full_s, send_s, center_s, edge_s, taps_s, own_s, kern_s, kernx_s,
            weight_s, weightx_s, fields_s, charge_s,
            toep_s, image_s, tgt_s, qa_s, qb_s, rcomp_s, acc_s, adj_s, outsend_s, outrecv_s,
            msend, mrecv, esend, erecv, ksend, krecv, wsend, wrecv, osend, orecv):
@@ -157,9 +157,9 @@
     def build(group, base):
         for o in range(BY):
             moved = base if o == 0 else pltpu.roll(base, o, 1)
-            toep_s[group * 256 + o * 16 : group * 256 + o * 16 + 16, :] = moved.astype(BF)
-
-    build(0, own_s[0:16, :])
+            toep_s[group * 256 + o * 16 : group * 256 + o * 16 + 16, :] = moved
+
+    build(0, own_s[0:16, :].astype(BF))
 
     for d in range(1, R):
         rr = lax.rem(r + d, R)
@@ -196,9 +196,9 @@
                 else:
                     tgt_s[pl.ds(TR * rr * 8 + g, TR, stride=8), :] = moved[:, :128]
 
-    def pack(n, carry):
-        base = pl.multiple_of(n * 128, 128)
-        rows = image_s[pl.ds(base, 22 * 8), :]
+    def pack(n):
+        base = n * 128
+        rows = image_s[base : base + 22 * 8, :]
         lane = lane_of((17 * 8, 128))
 
         def slot(s, by):
@@ -212,19 +212,21 @@
             jnp.where(lane < 4 * SLOT - 128, slot(3, 3 * SLOT - 128),
                       jnp.where(lane < 5 * SLOT - 128, slot(4, 4 * SLOT - 128), 0.0)))
         value = jnp.concatenate([low, high], axis=1)
-        qa_s[pl.ds(base, 128), :] = value[:128].astype(BF)
-        qb_s[pl.ds(base, 128), :] = value[8:].astype(BF)
-        return carry
-
-    lax.fori_loop(0, (NX + 32) // 16, pack, 0)
+        qa_s[base : base + 128, :] = value[:128].astype(BF)
+        qb_s[base : base + 128, :] = value[8:].astype(BF)
+
+    packs = (NX + 32) // 16
+    ready = (CHUNK + 32) // 16
+    for n in range(ready):
+        pack(n)
 
     kcopy.wait_recv()
     wcopy.wait_recv()
     theirs = kernx_s[:, 0:WIDE].astype(F32)
     rest = kernx_s[:, WIDE:].astype(F32)
-    build(1, jnp.concatenate([own_s[16:24, :], theirs[0:8]], axis=0))
-    build(2, jnp.concatenate(
-        [theirs[8:16], jnp.concatenate([rest[0:8], rest[8:16]], axis=1)], axis=0))
+    mixed = jnp.concatenate([own_s[16:24, :], theirs[0:8]], axis=0).astype(BF)
+    distant = jnp.concatenate(
+        [theirs[8:16], jnp.concatenate([rest[0:8], rest[8:16]], axis=1)], axis=0).astype(BF)
 
     lane8 = lane_of((8, 128))
     mine, other_w = weight_s[...], weightx_s[...]
@@ -248,7 +250,7 @@
     live = ((lane_of((PART, 128)) < BY) & (group_at < groups)
             & (field_col >= 0) & (field_col < C * TC))
 
-    def forward(n):
+    def forward(n, group):
         row0 = n * M
         pieces = []
         for t in range(STEPS):
@@ -256,13 +258,12 @@
             at = row0 + (TALL * t - t % 2) * 8
             pieces.append(source[at : at + M, :])
         patches = jnp.concatenate(pieces, axis=1)
-        for group in range(3):
-            fields_s[row0 : row0 + M, group * 256 : (group + 1) * 256] = lax.dot_general(
-                patches, toep_s[group * 256 : (group + 1) * 256, :],
-                (((1,), (1,)), ((), ())), preferred_element_type=F32)
-
-    def middle(n):
-        for at in range(n * M, (n + 1) * M, PART):
+        fields_s[row0 : row0 + M, group * 256 : (group + 1) * 256] = lax.dot_general(
+            patches, toep_s[group * 256 : (group + 1) * 256, :],
+            (((1,), (1,)), ((), ())), preferred_element_type=F32)
+
+    def middle(at):
+        if True:
             rows = slice(at, at + PART)
             power = None
             for group in range(3):
@@ -279,12 +280,11 @@
                 charge_s[rows, cols] = (
                     2.0 * weights[group] * wide * fields_s[rows, cols]).astype(BF)
 
-    def backward(n):
-        for t in range(STEPS):
-            at = n * M + TALL * t * 8
-            acc_s[at : at + M, :] += jnp.dot(
-                charge_s[n * M : (n + 1) * M, :], toep_s[:, t * 256 : (t + 1) * 256],
-                preferred_element_type=F32)
+    def backward(n, t):
+        at = n * M + TALL * t * 8
+        acc_s[at : at + M, :] += jnp.dot(
+            charge_s[n * M : (n + 1) * M, :], toep_s[:, t * 256 : (t + 1) * 256],
+            preferred_element_type=F32)
 
     fold = 128 // ST
     piece_rows = TR // fold
@@ -315,21 +315,10 @@
         outrecv_s[part, me] = outsend_s[part, r]
         return copies
 
-    chunks = NX // CHUNK
-    forward(0)
-    for n in range(chunks):
-        if n + 1 < chunks:
-            forward(n + 1)
-        middle(n)
-        if n + 1 < chunks:
-            backward(n)
-    ocopies = send_out(0, rcomp_s, HALF)
-    backward(chunks - 1)
-
-    def unpack(n, carry):
-        base = pl.multiple_of((n * 16 + HALF - 4) * 8, 8)
-        low = acc_s[pl.ds(base, 20 * 8), 0:128]
-        high = acc_s[pl.ds(base, 20 * 8), 128:256]
+    def unpack(n):
+        base = (n * 16 + HALF - 4) * 8
+        low = acc_s[base : base + 20 * 8, 0:128]
+        high = acc_s[base : base + 20 * 8, 128:256]
         lane = lane_of((128, 128))
 
         def slot(value, s, by):
@@ -340,11 +329,48 @@
                         slot(high, 2, 128 - 2 * SLOT))
         total = (slot(low, 0, 0) + slot(low, 1, 128 - SLOT) + two
                  + slot(high, 3, 256 - 3 * SLOT) + slot(high, 4, 256 - 4 * SLOT))
-        adj_s[pl.ds(pl.multiple_of(n * 128, 128), 128), :] = jnp.where(lane < SLOT, total, 0.0)
-        return carry
-
-    lax.fori_loop(0, NX // 16, unpack, 0)
-
+        adj_s[n * 128 : (n + 1) * 128, :] = jnp.where(lane < SLOT, total, 0.0)
+
+    def interleave(*lists):
+        order = sorted((((i + 0.5) / len(steps), n, i) for n, steps in enumerate(lists)
+                        for i in range(len(steps))))
+        for _, n, i in order:
+            lists[n][i]()
+
+    chunks = NX // CHUNK
+    call = functools.partial
+
+    def forwards(n):
+        return [call(forward, n, group) for group in range(3)]
+
+    def middles(n):
+        return [call(middle, at) for at in range(n * M, (n + 1) * M, PART)]
+
+    def backwards(n):
+        return [call(backward, n, t) for t in range(STEPS)]
+
+    def unpacks(n):
+        def done(m):
+            return NX // 16 if m == chunks - 1 else max(0, ((m + 1) * CHUNK - HALF) // 16)
+        low = done(n - 1) if n > 0 else 0
+        return [call(unpack, i) for i in range(low, done(n))]
+
+    forward(0, 0)
+    build(1, mixed)
+    forward(0, 1)
+    build(2, distant)
+    forward(0, 2)
+    for n in range(ready, packs):
+        pack(n)
+    interleave(middles(0), *([forwards(1)] if chunks > 1 else []))
+    for n in range(chunks - 1):
+        more = forwards(n + 2) if n + 2 < chunks else []
+        interleave(backwards(n) + more, middles(n + 1))
+    ocopies = send_out(0, rcomp_s, HALF)
+    spare = [step for n in range(chunks - 1) for step in unpacks(n)]
+    interleave(backwards(chunks - 1), spare)
+    for step in unpacks(chunks - 1):
+        step()
     ocopies += send_out(1, adj_s, 2 * HALF)
 
     def receive(part):
@@ -369,10 +395,10 @@
                     value = value if by == 0 else pltpu.roll(value, by, 1)
                     merged = value if m == 0 else jnp.where(lane < m * ST, merged, value)
                 if part == 0:
-                    resist_ref[rows, cols] = merged
+                    out_ref[0, rows, cols] = merged
                 else:
                     mask = full_s[rows, cols]
-                    grad_ref[rows, cols] = merged * mask * (1.0 - mask)
+                    out_ref[1, rows, cols] = merged * mask * (1.0 - mask)
 
     for copy in mcopies + ocopies:
         copy.wait_send()
@@ -393,12 +419,12 @@
     fold = 128 * G // TC
     vmem = pl.BlockSpec(memory_space=pltpu.VMEM)
     ends = 2 * max(1, R)
-    out = jax.ShapeDtypeStruct((TR, TC), F32)
-    return pl.pallas_call(
+    out = jax.ShapeDtypeStruct((2, TR, TC), F32)
+    both = pl.pallas_call(
         functools.partial(kernel, R, C, KN),
-        out_shape=(out, out),
+        out_shape=out,
         in_specs=[vmem] * 5,
-        out_specs=(vmem, vmem),
+        out_specs=vmem,
         scratch_shapes=[
             pltpu.VMEM((TR, TC), F32),
             pltpu.VMEM((2, TR, TC), BF),
@@ -436,6 +462,7 @@
         compiler_params=pltpu.CompilerParams(
             collective_id=0, has_side_effects=True, vmem_limit_bytes=48 * 1024 * 1024),
     )(mask_levels, level_offset, target_bits, socs_kernels, kernel_weights[None])
+    return (both[0], both[1])
 
 
 def solution(mesh):

time: 24.5 us -> 22.7 us (0.927)
  Pallas kernels: 21.3 us -> 20.1 us
  local copies, waits for them, and re-layouts: 2.31 us -> 1.71 us
    unnamed x11 -> x9, local copies, waits for them, and re-layouts: 2.31 us -> 1.05 us
    pallas_call x1, Pallas kernels: 21.3 us -> 20.1 us  [per_device(): pl.pallas_call(functools.partial(kernel, R, C, KN), out_shape=out, in_spe...]
    squeeze x0 -> x1, local copies, waits for them, and re-layouts: none -> 0.66 us  [per_device(): return (both[0], both[1])]
where the time goes in v2:
time: 22.7 us; the launch traced here: 22.6 us
  Pallas kernels  20.1 us (89%)
  local copies, waits for them, and re-layouts  1.71 us (8%)
  between operations  0.71 us (3%)
    pallas_call x1, Pallas kernels, per_device(): pl.pallas_call(functools.partial(kernel, R, C, KN), out_shape=out, in_spe...  20.1 us
    unnamed x9, local copies, waits for them, and re-layouts  1.05 us
    squeeze x1, local copies, waits for them, and re-layouts, per_device(): return (both[0], both[1])  0.66 us

profile of v2, /device:TPU:0, one launch (start us, length us, event | category | flops | bytes accessed | tf_op | source)
XLA Modules:
  0.0 22.6 jit_solution(9487274610853137335)
XLA Ops:
  0.6 0.0 copy-start
  0.6 0.0 copy-start.1
  0.7 0.0 copy-start.2
  0.7 0.0 copy-start.3
  0.7 1.0 %copy.7.kern_ref = bf16[2,12,35,35]{3,2,1,0:T(8,128)(2,1)S(1)} copy(bf16[2,12,35,35]{3,0,2,1:T(2,128)(2,1)} %param.8) | data formatting | bytes 117600 | tf_op args[3]
  1.7 0.0 copy-done
  1.7 0.0 copy-done.1
  1.7 0.0 copy-done.2
  1.7 0.0 copy-done.3
  1.8 20.1 %shard_map.68 = f32[2,32,512]{2,1,0:T(8,128)S(1)} custom-call(s32[32,512]{1,0:T(8,128)S(1)} %copy-done, f32[32,512]{1,0:T(8,128)S(1)} %copy-done.1, s32[32,512]{1,0:T(8,128)S(1)} %copy-done.2, bf16[2,12,35,35]{3,2,1,0:T(8,128)(2,1)S(1)} %copy.7.kern_ref, f32[1,12]{1,0:T(1,128)S(1)} %bitcast.5), custom_call_target="tpu_custom_call" | custom-call | tf_op jit(solution)/shard_map/pallas_call | solution.py:423
  21.9 0.7 %slice_bitcast_fusion = (f32[32,512]{1,0:T(8,128)}, f32[32,512]{1,0:T(8,128)}) fusion(f32[2,32,512]{2,1,0:T(8,128)S(1)} %shard_map.68), kind=kLoop, calls=%fused_computation | loop fusion | bytes 262144 | tf_op jit(solution)/shard_map/squeeze | solution.py:465
Async XLA Ops:
  0.6 1.1 %copy-start = (s32[32,512]{1,0:T(8,128)S(1)}, s32[32,512]{1,0:T(8,128)}, u32[]{:S(2)}) copy-start(s32[32,512]{1,0:T(8,128)} %levels_ref.1) | copy-start | bytes 196612
  0.6 1.1 %copy-start.1 = (f32[32,512]{1,0:T(8,128)S(1)}, f32[32,512]{1,0:T(8,128)}, u32[]{:S(2)}) copy-start(f32[32,512]{1,0:T(8,128)} %offset_ref.1) | copy-start | bytes 196612
  0.7 1.1 %copy-start.2 = (s32[32,512]{1,0:T(8,128)S(1)}, s32[32,512]{1,0:T(8,128)}, u32[]{:S(2)}) copy-start(s32[32,512]{1,0:T(8,128)} %target_ref.1) | copy-start | bytes 196612
  0.7 1.1 %copy-start.3 = (f32[12]{0:T(128)S(1)}, f32[12]{0:T(128)}, u32[]{:S(2)}) copy-start(f32[12]{0:T(128)} %param.9) | copy-start | bytes 148

commit v3 on v2

--- a/solution.py
+++ b/solution.py
@@ -85,40 +85,6 @@
     send_s[1] = target_ref[...].astype(F32).astype(BF)
     weight_s[...] = jnp.zeros((8, 128), F32)
     weight_s[0:1, 0:HALF_K] = weight_ref[...]
-
-    pl.semaphore_wait(barrier, waits)
-
-    def window(i):
-        tile = (ST * i + lead) // 128
-        return pl.multiple_of((jnp.clip(tile, 1, tiles - 1) - 1) * 128, 128)
-
-    other = (r, c, 1 - k)
-    kcopy = pltpu.make_async_remote_copy(kern_s, kernx_s, ksend, krecv,
-                                         device_id=other, device_id_type=MESH)
-    wcopy = pltpu.make_async_remote_copy(weight_s, weightx_s, wsend, wrecv,
-                                         device_id=other, device_id_type=MESH)
-    mcopies = []
-    for d in range(1, R):
-        rr = lax.rem(r + d, R)
-        copy = pltpu.make_async_remote_copy(
-            send_s.at[:, :, pl.ds(window(k * R + rr), 256)], center_s.at[r],
-            msend.at[d - 1], mrecv.at[r], device_id=(rr, c, k), device_id_type=MESH)
-        copy.start()
-        mcopies.append(copy)
-
-    def edge_copy(i, step, n, sender_row):
-        low = TC - 128 if step == 1 else 0
-        return pltpu.make_async_remote_copy(
-            send_s.at[:, :, pl.ds(low, 128)], edge_s.at[sender_row],
-            esend.at[n], erecv.at[sender_row],
-            device_id=(i % R, c + step, i // R), device_id_type=MESH)
-
-    edges = [(i, 1) for i in first] + [(i, -1) for i in last]
-    for n, (i, step) in enumerate(edges):
-        @pl.when((c + step >= 0) & (c + step < C) & (k == i // R))
-        def _():
-            edge_copy(i, step, n, r).start()
-    wcopy.start()
 
     WIDE = STEPS * 256
     taps_s[...] = jnp.zeros(taps_s.shape, F32)
@@ -146,6 +112,40 @@
     kern_s[:, 0:WIDE] = own_s[0:16, :].astype(BF)
     kern_s[:, WIDE:] = jnp.concatenate(
         [own_s[16:24, : WIDE // 2], own_s[16:24, WIDE // 2 :]], axis=0).astype(BF)
+
+    pl.semaphore_wait(barrier, waits)
+
+    def window(i):
+        tile = (ST * i + lead) // 128
+        return pl.multiple_of((jnp.clip(tile, 1, tiles - 1) - 1) * 128, 128)
+
+    other = (r, c, 1 - k)
+    kcopy = pltpu.make_async_remote_copy(kern_s, kernx_s, ksend, krecv,
+                                         device_id=other, device_id_type=MESH)
+    wcopy = pltpu.make_async_remote_copy(weight_s, weightx_s, wsend, wrecv,
+                                         device_id=other, device_id_type=MESH)
+    mcopies = []
+    for d in range(1, R):
+        rr = lax.rem(r + d, R)
+        copy = pltpu.make_async_remote_copy(
+            send_s.at[:, :, pl.ds(window(k * R + rr), 256)], center_s.at[r],
+            msend.at[d - 1], mrecv.at[r], device_id=(rr, c, k), device_id_type=MESH)
+        copy.start()
+        mcopies.append(copy)
+
+    def edge_copy(i, step, n, sender_row):
+        low = TC - 128 if step == 1 else 0
+        return pltpu.make_async_remote_copy(
+            send_s.at[:, :, pl.ds(low, 128)], edge_s.at[sender_row],
+            esend.at[n], erecv.at[sender_row],
+            device_id=(i % R, c + step, i // R), device_id_type=MESH)
+
+    edges = [(i, 1) for i in first] + [(i, -1) for i in last]
+    for n, (i, step) in enumerate(edges):
+        @pl.when((c + step >= 0) & (c + step < C) & (k == i // R))
+        def _():
+            edge_copy(i, step, n, r).start()
+    wcopy.start()
     kcopy.start()
 
     center_s[r] = send_s[:, :, pl.ds(window(me), 256)]

time: 22.7 us -> 22.6 us (level)
  no operation moved by 1% of the time
where the time goes in v3:
time: 22.6 us; the launch traced here: 22.5 us
  Pallas kernels  20.1 us (89%)
  local copies, waits for them, and re-layouts  1.71 us (8%)
  between operations  0.71 us (3%)
    pallas_call x1, Pallas kernels, per_device(): pl.pallas_call(functools.partial(kernel, R, C, KN), out_shape=out, in_spe...  20.1 us
    unnamed x9, local copies, waits for them, and re-layouts  1.05 us
    squeeze x1, local copies, waits for them, and re-layouts, per_device(): return (both[0], both[1])  0.66 us

profile of v3, /device:TPU:0, one launch (start us, length us, event | category | flops | bytes accessed | tf_op | source)
XLA Modules:
  0.0 22.5 jit_solution(16322259571678310566)
XLA Ops:
  0.6 0.0 copy-start
  0.6 0.0 copy-start.1
  0.7 0.0 copy-start.2
  0.7 0.0 copy-start.3
  0.7 1.0 %copy.7.kern_ref = bf16[2,12,35,35]{3,2,1,0:T(8,128)(2,1)S(1)} copy(bf16[2,12,35,35]{3,0,2,1:T(2,128)(2,1)} %param.8) | data formatting | bytes 117600 | tf_op args[3]
  1.7 0.0 copy-done
  1.7 0.0 copy-done.1
  1.7 0.0 copy-done.2
  1.7 0.0 copy-done.3
  1.8 20.1 %shard_map.68 = f32[2,32,512]{2,1,0:T(8,128)S(1)} custom-call(s32[32,512]{1,0:T(8,128)S(1)} %copy-done, f32[32,512]{1,0:T(8,128)S(1)} %copy-done.1, s32[32,512]{1,0:T(8,128)S(1)} %copy-done.2, bf16[2,12,35,35]{3,2,1,0:T(8,128)(2,1)S(1)} %copy.7.kern_ref, f32[1,12]{1,0:T(1,128)S(1)} %bitcast.5), custom_call_target="tpu_custom_call" | custom-call | tf_op jit(solution)/shard_map/pallas_call | solution.py:423
  21.8 0.7 %slice_bitcast_fusion = (f32[32,512]{1,0:T(8,128)}, f32[32,512]{1,0:T(8,128)}) fusion(f32[2,32,512]{2,1,0:T(8,128)S(1)} %shard_map.68), kind=kLoop, calls=%fused_computation | loop fusion | bytes 262144 | tf_op jit(solution)/shard_map/squeeze | solution.py:465
Async XLA Ops:
  0.6 1.1 %copy-start = (s32[32,512]{1,0:T(8,128)S(1)}, s32[32,512]{1,0:T(8,128)}, u32[]{:S(2)}) copy-start(s32[32,512]{1,0:T(8,128)} %levels_ref.1) | copy-start | bytes 196612
  0.6 1.1 %copy-start.1 = (f32[32,512]{1,0:T(8,128)S(1)}, f32[32,512]{1,0:T(8,128)}, u32[]{:S(2)}) copy-start(f32[32,512]{1,0:T(8,128)} %offset_ref.1) | copy-start | bytes 196612
  0.7 1.1 %copy-start.2 = (s32[32,512]{1,0:T(8,128)S(1)}, s32[32,512]{1,0:T(8,128)}, u32[]{:S(2)}) copy-start(s32[32,512]{1,0:T(8,128)} %target_ref.1) | copy-start | bytes 196612
  0.7 1.1 %copy-start.3 = (f32[12]{0:T(128)S(1)}, f32[12]{0:T(128)}, u32[]{:S(2)}) copy-start(f32[12]{0:T(128)} %param.9) | copy-start | bytes 148
